TPU v7x, 32 devices: a whole 2x2x4 slice. The times are simulated.
32 devices in a mesh: dp: 8 (over y, x, core), mp: 4 (over z).
Axes of the slice: x: 2, y: 2, z: 4, core: 2. Of those that a mesh axis runs over, the one named last changes fastest.
Arguments:
- inputs: bfloat16 [512, 65536], P('mp', 'dp'), may hold values from -24 to 24
- cotangent: bfloat16 [512, 65536], P('mp', 'dp'), may hold values from -4 to 4
- member_mask: int32 [2048, 32], P('dp'), may hold values from 0 to 1, as said below
- members: float32 [6, 32, 512], P(None, 'dp', 'mp'), may hold values from -3 to 3
- first_moment: float32 [6, 32, 512], P(None, 'dp', 'mp')
- second_moment: float32 [6, 32, 512], P(None, 'dp', 'mp'), as said below
- first_weight: float32 [512, 512], P('dp', 'mp'), may hold values from -0.25 to 0.25
- second_weight: float32 [512, 512], P('mp', 'dp'), may hold values from -0.25 to 0.25
- first_left: float32 [512, 512], P('dp', 'mp')
- first_right: float32 [512, 512], P('dp', 'mp')
- second_left: float32 [512, 512], P('mp', 'dp')
- second_right: float32 [512, 512], P('mp', 'dp')
- first_left_root: float32 [512, 512], P('dp')
- first_right_root: float32 [512, 512], P('mp')
- second_left_root: float32 [512, 512], P('mp')
- second_right_root: float32 [512, 512], P('dp')
Outputs:
- logits: bfloat16 [512, 65536], P('mp', 'dp')
- input_grad: bfloat16 [512, 65536], P('mp', 'dp')
- rms_stats: float32 [2], replicated
- first_grad: float32 [512, 512], P('dp', 'mp')
- first_new: float32 [512, 512], P('dp', 'mp')
- first_left_new: float32 [512, 512], P('dp', 'mp')
- first_right_new: float32 [512, 512], P('dp', 'mp')
- second_grad: float32 [512, 512], P('mp', 'dp')
- second_new: float32 [512, 512], P('mp', 'dp')
- second_left_new: float32 [512, 512], P('mp', 'dp')
- second_right_new: float32 [512, 512], P('mp', 'dp')
- moment_one_new: float32 [6, 32, 512], P(None, 'dp', 'mp')
- moment_two_new: float32 [6, 32, 512], P(None, 'dp', 'mp')
- members_new: float32 [6, 32, 512], P(None, 'dp', 'mp')
Inputs may be any that keep to these rules, and one draw needn't show every extreme that they name: `member_mask`: each object has between 8 and 32 trained members; some object has exactly 8 and some exactly 32. `second_moment`: positive.
All inputs are finite; a program needn't handle non-finite values.
Results may differ from a plain program's by a relative error of at most 0.0087.
Values may be sent and summed in bfloat16 or wider, within the bound.
A program may use at most 128 MiB of HBM per device.

v0:
```python
import jax
import jax.numpy as jnp
from jax import lax
from jax.sharding import PartitionSpec as P

D = 512
K = 32
STEP = 10
beta_first = 0.9
beta_second = 0.999
adam_eps = 1e-08
adam_rate = 0.2
stat_decay = 0.95
shampoo_rate = 1.0
over_rows = (((0,), (0,)), ((), ()))
over_cols = (((1,), (1,)), ((), ()))


def group_count(values):
    objects = values.shape[1] // K
    repeat = max(1, 128 // K)
    return repeat


def tiled_table(table, repeat):
    return jnp.tile(table.T, (1, repeat))


def by_member(values, table):
    width = values.shape[0]
    repeat = group_count(values)
    shaped = values.reshape(width, -1, repeat * K)
    return (shaped * tiled_table(table, repeat)[:, None, :]).reshape(values.shape)


def member_affine(values, gain, bias):
    width = values.shape[0]
    repeat = group_count(values)
    shaped = values.reshape(width, -1, repeat * K)
    return (
        shaped * tiled_table(gain, repeat)[:, None, :] + tiled_table(bias, repeat)[:, None, :]
    ).reshape(values.shape)


def member_sum(values):
    width = values.shape[0]
    repeat = group_count(values)
    partial_value = values.reshape(width, -1, repeat * K).sum(1)
    return partial_value.reshape(width, repeat, K).sum(1).T


def middle_forward(rows_in, first_low, second_low, gain_in, bias_in, row_mid):
    hidden_pre = lax.dot_general(first_low, rows_in, over_rows, preferred_element_type=jnp.float32)
    shifted = member_affine(hidden_pre, gain_in, bias_in)
    hidden, gelu_pull = jax.vjp(jax.nn.gelu, shifted)
    hidden_in = by_member(hidden, row_mid).astype(jnp.bfloat16)
    partial_value = lax.dot_general(
        second_low, hidden_in, over_rows, preferred_element_type=jnp.float32
    )
    return (hidden_pre, hidden, gelu_pull, hidden_in, partial_value)


def middle_backward(
    grad_rows,
    rows_in,
    first_low,
    second_low,
    gain_in,
    row_mid,
    hidden_pre,
    hidden,
    gelu_pull,
    hidden_in,
):
    grad_second = lax.dot_general(
        hidden_in, grad_rows, over_cols, preferred_element_type=jnp.float32
    )
    grad_hidin = jnp.dot(second_low, grad_rows, preferred_element_type=jnp.float32)
    grad_row_mid = member_sum(grad_hidin * hidden)
    grad_shift = gelu_pull(by_member(grad_hidin, row_mid))[0]
    grad_bias_in = member_sum(grad_shift)
    grad_gain_in = member_sum(grad_shift * hidden_pre)
    grad_pre = by_member(grad_shift, gain_in).astype(jnp.bfloat16)
    grad_first = lax.dot_general(rows_in, grad_pre, over_cols, preferred_element_type=jnp.float32)
    row_back = jnp.dot(first_low, grad_pre, preferred_element_type=jnp.float32)
    return (
        grad_first,
        grad_second,
        jnp.stack([grad_gain_in, grad_bias_in, grad_row_mid]),
        row_back,
    )


def on_device(
    inputs,
    cotangent,
    member_mask,
    members,
    first_moment,
    second_moment,
    first_weight,
    second_weight,
    first_left,
    first_right,
    second_left,
    second_right,
    first_left_root,
    first_right_root,
    second_left_root,
    second_right_root,
):
    high = lax.Precision.HIGHEST
    first_block, second_block, member_cols = (
        lax.all_gather(first_weight, "dp", axis=0, tiled=True),
        lax.all_gather(second_weight, "dp", axis=1, tiled=True),
        lax.all_gather(members, "dp", axis=1, tiled=True),
    )
    row_in = member_cols[0]
    gain_out = member_cols[4]
    bias_out = member_cols[5]
    values = inputs.astype(jnp.float32)
    weight_mask = member_mask.astype(jnp.float32).reshape(1, -1)
    scaled = by_member(values, row_in).astype(jnp.bfloat16)
    first_low = first_block.astype(jnp.bfloat16)
    second_low = second_block.astype(jnp.bfloat16)
    hidden_tables = member_cols[1:4]
    gathered = lax.all_gather(scaled, "mp", axis=0, tiled=True)
    hidden_pre, hidden, gelu_pull, hidden_in, partial_value = middle_forward(
        gathered, first_low, second_low, hidden_tables[0], hidden_tables[1], hidden_tables[2]
    )
    projected = lax.psum_scatter(partial_value, "mp", scatter_dimension=0, tiled=True)
    branch = member_affine(projected, gain_out, bias_out)
    logits = (values + branch).astype(jnp.bfloat16)
    first_column = (lax.axis_index("mp") == 0).astype(jnp.float32)
    totals = lax.psum(
        (
            jnp.sum(weight_mask * values * values),
            jnp.sum(weight_mask * branch * branch),
            jnp.sum(weight_mask) * first_column,
        ),
        ("dp", "mp"),
    )
    rms_stats = jnp.sqrt(jnp.stack([totals[0], totals[1]]) / (totals[2] * D))
    grad_out = cotangent.astype(jnp.float32) * weight_mask
    grad_bias_out = member_sum(grad_out)
    grad_gain_out = member_sum(grad_out * projected)
    grad_proj = by_member(grad_out, gain_out).astype(jnp.bfloat16)
    grad_full = lax.all_gather(grad_proj, "mp", axis=0, tiled=True)
    grad_first, grad_second, mid_grads, partial_back = middle_backward(
        grad_full,
        gathered,
        first_low,
        second_low,
        hidden_tables[0],
        hidden_tables[2],
        hidden_pre,
        hidden,
        gelu_pull,
        hidden_in,
    )
    grad_scaled = lax.psum_scatter(partial_back, "mp", scatter_dimension=0, tiled=True)
    grad_row_in = member_sum(grad_scaled * values)
    input_grad = (by_member(grad_scaled, row_in) + grad_out).astype(jnp.bfloat16)
    grad_vec = jnp.concatenate(
        [grad_row_in[None], mid_grads, grad_gain_out[None], grad_bias_out[None]], axis=0
    )
    first_grad, second_grad, vec_grad = (
        lax.psum_scatter(grad_first, "dp", scatter_dimension=0, tiled=True),
        lax.psum_scatter(grad_second, "dp", scatter_dimension=1, tiled=True),
        lax.psum_scatter(grad_vec, "dp", scatter_dimension=1, tiled=True),
    )
    first_rows, second_cols = (
        lax.all_gather(first_grad, "dp", axis=0, tiled=True),
        lax.all_gather(second_grad, "dp", axis=1, tiled=True),
    )
    first_total, second_total = (
        lax.all_gather(first_rows, "mp", axis=1, tiled=True),
        lax.all_gather(second_cols, "mp", axis=0, tiled=True),
    )
    owned = first_grad.shape[0]
    width = first_grad.shape[1]
    start_dp = lax.axis_index("dp") * owned
    start_mp = lax.axis_index("mp") * width
    left_rows = lax.dynamic_slice_in_dim(first_total, start_dp, owned, 0)
    right_rows = lax.dynamic_slice_in_dim(first_total, start_mp, width, 0)
    left_cols = lax.dynamic_slice_in_dim(first_total, start_dp, owned, 1)
    right_cols = lax.dynamic_slice_in_dim(first_total, start_mp, width, 1)
    first_left_new = stat_decay * first_left + (1.0 - stat_decay) * lax.dot_general(
        left_rows, right_rows, over_cols, precision=high
    )
    first_right_new = stat_decay * first_right + (1.0 - stat_decay) * lax.dot_general(
        left_cols, right_cols, over_rows, precision=high
    )
    first_step = lax.dot_general(
        jnp.dot(first_left_root, first_total, precision=high),
        first_right_root,
        over_cols,
        precision=high,
    )
    first_new = first_weight - shampoo_rate * first_step
    upper_rows = lax.dynamic_slice_in_dim(second_total, start_mp, width, 0)
    lower_rows = lax.dynamic_slice_in_dim(second_total, start_dp, owned, 0)
    upper_cols = lax.dynamic_slice_in_dim(second_total, start_mp, width, 1)
    lower_cols = lax.dynamic_slice_in_dim(second_total, start_dp, owned, 1)
    second_left_new = stat_decay * second_left + (1.0 - stat_decay) * lax.dot_general(
        upper_rows, lower_rows, over_cols, precision=high
    )
    second_right_new = stat_decay * second_right + (1.0 - stat_decay) * lax.dot_general(
        upper_cols, lower_cols, over_rows, precision=high
    )
    second_step = lax.dot_general(
        jnp.dot(second_left_root, second_total, precision=high),
        second_right_root,
        over_cols,
        precision=high,
    )
    second_new = second_weight - shampoo_rate * second_step
    moment_one = beta_first * first_moment + (1.0 - beta_first) * vec_grad
    moment_two = beta_second * second_moment + (1.0 - beta_second) * vec_grad * vec_grad
    corr_one = 1.0 - beta_first**STEP
    corr_two = 1.0 - beta_second**STEP
    members_new = members - adam_rate * (moment_one / corr_one) / (
        jnp.sqrt(moment_two / corr_two) + adam_eps
    )
    return (
        logits,
        input_grad,
        rms_stats,
        first_grad,
        first_new,
        first_left_new,
        first_right_new,
        second_grad,
        second_new,
        second_left_new,
        second_right_new,
        moment_one,
        moment_two,
        members_new,
    )


def solution(mesh):
    placed = (
        P("mp", "dp"),
        P("mp", "dp"),
        P("dp", None),
        P(None, "dp", "mp"),
        P(None, "dp", "mp"),
        P(None, "dp", "mp"),
        P("dp", "mp"),
        P("mp", "dp"),
        P("dp", "mp"),
        P("dp", "mp"),
        P("mp", "dp"),
        P("mp", "dp"),
        P("dp", None),
        P("mp", None),
        P("mp", None),
        P("dp", None),
    )
    return jax.shard_map(
        on_device,
        mesh=mesh,
        in_specs=placed,
        out_specs=(
            P("mp", "dp"),
            P("mp", "dp"),
            P(),
            P("dp", "mp"),
            P("dp", "mp"),
            P("dp", "mp"),
            P("dp", "mp"),
            P("mp", "dp"),
            P("mp", "dp"),
            P("mp", "dp"),
            P("mp", "dp"),
            P(None, "dp", "mp"),
            P(None, "dp", "mp"),
            P(None, "dp", "mp"),
        ),
        check_vma=False,
    )
```

profile of v0, /device:TPU:1, one launch (start us, length us, event | category | flops | bytes accessed | tf_op | source)
XLA Modules:
  0.0 1112.2 jit_solution(12044640973617156003)
XLA Ops:
  8.9 10.6 all_gather.27
  19.6 3.2 copy.41
  25.1 4.1 copy.39
  29.2 3.4 fusion.14
  32.7 9.2 all_gather.30
  41.9 8.2 all_gather.29
  50.1 124.2 %all-gather.7.cloned.1.call-done = bf16[512,8192]{0,1:T(8,128)(2,1)} async-done(((bf16[128,8192]{0,1:T(8,128)(2,1)}), bf16[512,8192]{0,1:T(8,128)(2,1)}) %all-gather.7.cloned.1.call-update) | async-done | bytes 8388624 | tf_op jit(solution)/shard_map/all_gather | solution.py:148
  174.3 7.8 convolution_bitcast_fusion.2
  182.1 141.2 %all-gather.5.cloned.1.call-done = bf16[512,8192]{0,1:T(8,128)(2,1)} async-done(((bf16[128,8192]{0,1:T(8,128)(2,1)}), bf16[512,8192]{0,1:T(8,128)(2,1)}) %all-gather.5.cloned.1.call-update) | async-done | bytes 8388624 | tf_op jit(solution)/shard_map/all_gather | solution.py:127
  323.3 10.1 fusion.42
  333.4 4.1 fusion.47
  337.7 2.4 fusion.10
  341.4 6.5 fusion.45
  348.0 20.8 %reduce-scatter.12.cloned.1.call-done = f32[128,64]{0,1:T(8,128)} async-done(((f32[128,512]{0,1:T(8,128)}), f32[128,64]{0,1:T(8,128)}) %reduce-scatter.12.cloned.1.call-update) | async-done | bytes 32784 | tf_op jit(solution)/shard_map/reduce_scatter | solution.py:169
  368.8 11.2 %all_gather.34 = f32[128,512]{0,1:T(8,128)} all-gather(f32[128,64]{0,1:T(8,128)} %reduce-scatter.12.cloned.1.call-done), channel_id=1, replica_groups=mesh['dp'=8,'mp'=4] {'dp'}, dimensions={1}, use_global_device_ids=true | all-gather | bytes 294912 | tf_op jit(solution)/shard_map/all_gather | solution.py:174
  380.1 26.1 %reduce-scatter.10.cloned.1.call-done = f32[64,128]{1,0:T(8,128)} async-done(((f32[512,128]{1,0:T(8,128)}), f32[64,128]{1,0:T(8,128)}) %reduce-scatter.10.cloned.1.call-update) | async-done | bytes 32784 | tf_op jit(solution)/shard_map/reduce_scatter | solution.py:168
  406.2 11.2 %all_gather.32 = f32[512,128]{1,0:T(8,128)} all-gather(f32[64,128]{1,0:T(8,128)} %reduce-scatter.10.cloned.1.call-done), channel_id=1, replica_groups=mesh['dp'=8,'mp'=4] {'dp'}, dimensions={0}, use_global_device_ids=true | all-gather | bytes 294912 | tf_op jit(solution)/shard_map/all_gather | solution.py:173
  417.4 9.6 convolution_bitcast_fusion
  427.2 8.1 convolution_bitcast_fusion.1
  438.4 2.4 reduce_sum.140
  440.9 2.4 reduce_sum.144
  443.3 2.6 reduce_sum.142
  446.0 2.4 fusion.19
  450.5 16.5 %all-gather.9.cloned.1.call-done = f32[512,512]{1,0:T(8,128)} async-done(((f32[512,128]{1,0:T(8,128)}), f32[512,512]{1,0:T(8,128)}) %all-gather.9.cloned.1.call-update) | async-done | bytes 1048592 | tf_op jit(solution)/shard_map/all_gather | solution.py:177
  477.8 271.4 %reduce-scatter.8.cloned.1.call-done = f32[128,8192]{0,1:T(8,128)} async-done(((f32[512,8192]{0,1:T(8,128)}), f32[128,8192]{0,1:T(8,128)}) %reduce-scatter.8.cloned.1.call-update) | async-done | bytes 4194320 | tf_op jit(solution)/shard_map/reduce_scatter | solution.py:161
  749.2 283.4 %reduce-scatter.6.cloned.1.call-done = f32[128,8192]{0,1:T(8,128)} async-done(((f32[512,8192]{0,1:T(8,128)}), f32[128,8192]{0,1:T(8,128)}) %reduce-scatter.6.cloned.1.call-update) | async-done | bytes 4194320 | tf_op jit(solution)/shard_map/reduce_scatter | solution.py:131
  1032.6 10.3 convert_multiply_fusion
  1047.8 2.6 reduce_sum.148
  1051.1 40.9 %all-reduce.1 = (f32[1]{0:T(128)}, f32[1]{0:T(128)}, f32[]{:T(128)}) all-reduce(f32[1]{0:T(128)} %bitcast.29, f32[1]{0:T(128)} %bitcast.28, f32[]{:T(128)S(6)} %mul.263), channel_id=1, replica_groups=mesh['dp'=8,'mp'=4] {'dp','mp'}, use_global_device_ids=true, to_apply=%region_5.0 | all-reduce | flops 3 | bytes 24 | tf_op jit(solution)/shard_map/psum | solution.py:135
  1094.6 4.1 copy.44
  1098.7 2.9 copy.43
  1101.6 2.7 all-reduce.4.cloned.1.call-done
  (100 shorter events, 29.5 us)
Async XLA Ops:
  7.2 464.1 %copy-start = (f32[128,512]{1,0:T(8,128)S(1)}, f32[128,512]{1,0:T(8,128)}, u32[]{:S(2)}) copy-start(f32[128,512]{1,0:T(8,128)} %param.30) | copy-start | bytes 786436
  7.2 167.1 %all-gather.7.cloned.1.call-start = ((), (), s32[]{:S(2)}) async-start(), calls=%async_computation.6 | async-start | bytes 10485760 | tf_op jit(solution)/shard_map/all_gather | solution.py:148
  22.8 6.4 copy-start.2
  25.1 298.1 %all-gather.5.cloned.1.call-start = ((), (), s32[]{:S(2)}) async-start(), calls=%async_computation.4 | async-start | bytes 10485760 | tf_op jit(solution)/shard_map/all_gather | solution.py:127
  29.2 3.5 copy-start.9
  29.2 3.5 copy-start.8
  32.6 336.2 %reduce-scatter.12.cloned.1.call-start = ((), (), s32[]{:S(2)}) async-start(), calls=%async_computation.10 | async-start | bytes 294912 | tf_op jit(solution)/shard_map/reduce_scatter | solution.py:169
  323.3 10.1 copy-start.1
  337.5 68.7 %reduce-scatter.10.cloned.1.call-start = ((), (), s32[]{:S(2)}) async-start(), calls=%async_computation.8 | async-start | bytes 294912 | tf_op jit(solution)/shard_map/reduce_scatter | solution.py:168
  340.1 1.3 copy-start.4
  348.0 98.0 %all-gather.11.cloned.1.call-start = ((), (), s32[]{:S(2)}) async-start(), calls=%async_computation.11 | async-start | bytes 1310720 | tf_op jit(solution)/shard_map/all_gather | solution.py:178
  380.0 86.9 %all-gather.9.cloned.1.call-start = ((), (), s32[]{:S(2)}) async-start(), calls=%async_computation.9 | async-start | bytes 1310720 | tf_op jit(solution)/shard_map/all_gather | solution.py:177
  417.4 331.8 %reduce-scatter.8.cloned.1.call-start = ((), (), s32[]{:S(2)}) async-start(), calls=%async_computation.7 | async-start | bytes 20971520 | tf_op jit(solution)/shard_map/reduce_scatter | solution.py:161
  427.1 605.5 %reduce-scatter.6.cloned.1.call-start = ((), (), s32[]{:S(2)}) async-start(), calls=%async_computation.5 | async-start | bytes 20971520 | tf_op jit(solution)/shard_map/reduce_scatter | solution.py:131
  435.2 0.7 copy-start.20
  435.2 1.9 copy-start.12
  435.3 669.0 %all-reduce.4.cloned.1.call-start = ((), (), s32[]{:S(2)}) async-start(), calls=%async_computation.12 | async-start | bytes 196608
  440.8 5.2 copy-start.16
  440.8 7.6 copy-start.14
  440.8 26.1 %copy-start.15 = (f32[64,128]{1,0:T(8,128)S(1)}, f32[64,128]{1,0:T(8,128)}, u32[]{:S(2)}) copy-start(f32[64,128]{1,0:T(8,128)} %param.24) | copy-start | bytes 98308
  440.8 28.1 %copy-start.17 = (f32[64,128]{1,0:T(8,128)S(1)}, f32[64,128]{1,0:T(8,128)}, u32[]{:S(2)}) copy-start(f32[64,128]{1,0:T(8,128)} %param.25) | copy-start | bytes 98308
  443.3 30.3 %copy-start.10 = (f32[64,512]{1,0:T(8,128)S(1)}, f32[64,512]{1,0:T(8,128)}, u32[]{:S(2)}) copy-start(f32[64,512]{1,0:T(8,128)} %param.31) | copy-start | bytes 393220
  443.3 31.2 %copy-start.11 = (f32[64,512]{1,0:T(8,128)S(1)}, f32[64,512]{1,0:T(8,128)}, u32[]{:S(2)}) copy-start(f32[64,512]{1,0:T(8,128)} %param.28) | copy-start | bytes 393220
  443.3 33.4 %copy-start.6 = (f32[128,512]{1,0:T(8,128)S(1)}, f32[128,512]{1,0:T(8,128)}, u32[]{:S(2)}) copy-start(f32[128,512]{1,0:T(8,128)} %param.29) | copy-start | bytes 786436
  443.3 589.3 %copy-start.3 = (bf16[128,8192]{0,1:T(8,128)(2,1)S(1)}, bf16[128,8192]{0,1:T(8,128)(2,1)}, u32[]{:S(2)}) copy-start(bf16[128,8192]{0,1:T(8,128)(2,1)} %copy-done.2) | copy-start | bytes 6291460
  1047.8 50.9 %copy-start.5 = (bf16[128,8192]{0,1:T(8,128)(2,1)S(1)}, bf16[128,8192]{0,1:T(8,128)(2,1)}, u32[]{:S(2)}) copy-start(bf16[128,8192]{0,1:T(8,128)(2,1)} %get-tuple-element.73) | copy-start | bytes 6291460
  1050.5 0.6 copy-start.7
  1094.6 9.7 copy-start.13
  1094.6 9.7 copy-start.18
  1094.6 9.7 copy-start.19
Sparse Core Ops, SparseCore 0:
  25.2 149.0 all-gather.6
  175.9 147.3 all-gather.4
  337.6 31.1 reduce-scatter.11
  372.6 33.5 reduce-scatter.9
  407.6 29.3 all-gather.10
  438.4 28.4 all-gather.8
  469.3 279.8 reduce-scatter.7
  751.7 280.9 reduce-scatter.5
  1051.2 52.9 all-reduce.3
where the time goes:
time: 1110 us
  waiting for transfers between devices  886 us (80%)
  blocking collectives  91.3 us (8%)
  matrix products  61.4 us (6%)
  other arithmetic  37.9 us (3%)
  local copies, waits for them, and re-layouts  18.3 us (2%)
  between operations  16.2 us (1%)
    reduce_scatter x1, waiting for transfers between devices, on_device(): lax.psum_scatter(partial_value, 'mp', scatter_dimension=0, tiled=True)  283 us
    reduce_scatter x1, waiting for transfers between devices, on_device(): lax.psum_scatter(partial_back, 'mp', scatter_dimension=0, tiled=True)  271 us
    all_gather x1, waiting for transfers between devices, on_device(): gathered = lax.all_gather(scaled, 'mp', axis=0, tiled=True)  141 us
    all_gather x1, waiting for transfers between devices, on_device(): grad_full = lax.all_gather(grad_proj, 'mp', axis=0, tiled=True)  124 us
    psum x1, blocking collectives, on_device(): lax.psum((jnp.sum(weight_mask * values * values), jnp.sum(weight_mask * b...  40.9 us
    reduce_scatter x1, waiting for transfers between devices, on_device(): lax.psum_scatter(grad_first, 'dp', scatter_dimension=0, tiled=True)  26.1 us
  transfers between devices with their start and end apart: 9, of which 8 were waited for; matrix products, arithmetic and copies ran while one was open for 7% of the time, Pallas kernels for 0%

commit v1 on v0

--- a/solution.py
+++ b/solution.py
@@ -145,7 +145,14 @@
     grad_bias_out = member_sum(grad_out)
     grad_gain_out = member_sum(grad_out * projected)
     grad_proj = by_member(grad_out, gain_out).astype(jnp.bfloat16)
-    grad_full = lax.all_gather(grad_proj, "mp", axis=0, tiled=True)
+    ways, here, step = (lax.axis_size("mp"), lax.axis_index("mp"), grad_proj.shape[0])
+    line, have = (grad_proj, 1)
+    while have < ways:
+        line = jnp.concatenate(
+            [line, lax.ppermute(line, "mp", [(d, (d - have) % ways) for d in range(ways)])], axis=0
+        )
+        have = 2 * have
+    grad_full = jnp.roll(line, here * step, axis=0)
     grad_first, grad_second, mid_grads, partial_back = middle_backward(
         grad_full,
         gathered,

time: 1110 us -> 1210 us (1.090)
  waiting for transfers between devices: 886 us -> 958 us
  local copies, waits for them, and re-layouts: 18.3 us -> 36 us
    ppermute x0 -> x2, waiting for transfers between devices: none -> 337 us  [on_device(): lax.ppermute(line, 'mp', [(d, (d - have) % ways) for d in range(ways)])]
    all_gather x1, waiting for transfers between devices: 141 us -> 0.01 us  [on_device(): gathered = lax.all_gather(scaled, 'mp', axis=0, tiled=True)]
    all_gather x1 -> x0, waiting for transfers between devices: 124 us -> none  [on_device(): grad_full = lax.all_gather(grad_proj, 'mp', axis=0, tiled=True)]
    unnamed x53 -> x67, local copies, waits for them, and re-layouts: 18 us -> 31.2 us
  transfers between devices with their start and end apart: 9 -> 10, of which waited for: 8 -> 8; matrix products, arithmetic and copies ran while one was open for 7% -> 7% of each run, Pallas kernels for 0% -> 0%
where the time goes in v1:
time: 1210 us; the launch traced here: 1200 us
  waiting for transfers between devices  958 us (79%)
  blocking collectives  93.3 us (8%)
  matrix products  57.2 us (5%)
  other arithmetic  38.6 us (3%)
  local copies, waits for them, and re-layouts  36 us (3%)
  between operations  16.6 us (1%)
    ppermute x2, waiting for transfers between devices, on_device(): lax.ppermute(line, 'mp', [(d, (d - have) % ways) for d in range(ways)])  337 us
    reduce_scatter x1, waiting for transfers between devices, on_device(): lax.psum_scatter(partial_value, 'mp', scatter_dimension=0, tiled=True)  284 us
    reduce_scatter x1, waiting for transfers between devices, on_device(): lax.psum_scatter(partial_back, 'mp', scatter_dimension=0, tiled=True)  271 us
    psum x1, blocking collectives, on_device(): lax.psum((jnp.sum(weight_mask * values * values), jnp.sum(weight_mask * b...  40.9 us
    unnamed x67, local copies, waits for them, and re-layouts  31.2 us
    reduce_scatter x1, waiting for transfers between devices, on_device(): lax.psum_scatter(grad_first, 'dp', scatter_dimension=0, tiled=True)  26.2 us
  transfers between devices with their start and end apart: 10, of which 8 were waited for; matrix products, arithmetic and copies ran while one was open for 7% of the time, Pallas kernels for 0%

profile of v1, /device:TPU:1, one launch (start us, length us, event | category | flops | bytes accessed | tf_op | source)
XLA Modules:
  0.0 1204.0 jit_solution(12287127302281008612)
XLA Ops:
  8.0 10.5 all_gather.24
  18.6 3.2 copy.39
  24.1 3.2 copy.41
  29.8 3.3 collective-permute-start
  33.1 109.7 %collective-permute-done = bf16[128,8192]{0,1:T(8,128)(2,1)S(1)} collective-permute-done((bf16[128,8192]{0,1:T(8,128)(2,1)S(1)}, bf16[128,8192]{0,1:T(8,128)(2,1)S(1)}, u32[]{:S(2)}, u32[]{:S(2)}) %collective-permute-start) | collective-permute-done | bytes 2097184 | tf_op jit(solution)/shard_map/ppermute | solution.py:152
  142.8 2.6 pad_maximum_fusion
  145.5 9.6 all_gather.27
  155.1 9.9 all_gather.26
  164.9 3.3 constant_dynamic-update-slice_fusion.4
  168.2 227.8 %collective-permute-done.1 = bf16[256,8192]{0,1:T(8,128)(2,1)} collective-permute-done((bf16[256,8192]{0,1:T(8,128)(2,1)}, bf16[256,8192]{0,1:T(8,128)(2,1)}, u32[]{:S(2)}, u32[]{:S(2)}) %collective-permute-start.1) | collective-permute-done | bytes 4194336 | tf_op jit(solution)/shard_map/ppermute | solution.py:152
  396.1 4.6 constant_dynamic-update-slice_fusion.3
  404.6 4.6 constant_dynamic-update-slice_fusion
  409.1 5.9 convolution_bitcast_fusion.3
  417.3 7.7 fusion.47
  425.0 4.2 fusion
  433.2 6.5 fusion.50
  439.8 20.4 %reduce-scatter.12.cloned.1.call-done = f32[128,64]{0,1:T(8,128)} async-done(((f32[128,512]{0,1:T(8,128)}), f32[128,64]{0,1:T(8,128)}) %reduce-scatter.12.cloned.1.call-update) | async-done | bytes 32784 | tf_op jit(solution)/shard_map/reduce_scatter | solution.py:176
  460.2 11.2 all_gather.30
  471.5 26.2 %reduce-scatter.10.cloned.1.call-done = f32[64,128]{1,0:T(8,128)} async-done(((f32[512,128]{1,0:T(8,128)}), f32[64,128]{1,0:T(8,128)}) %reduce-scatter.10.cloned.1.call-update) | async-done | bytes 32784 | tf_op jit(solution)/shard_map/reduce_scatter | solution.py:175
  497.7 11.2 all_gather.28
  509.0 9.7 convolution_bitcast_fusion
  518.7 8.1 convolution_bitcast_fusion.1
  534.9 2.7 reduce_sum.142
  541.9 16.5 %all-gather.6.cloned.1.call-done = f32[512,512]{1,0:T(8,128)} async-done(((f32[512,128]{1,0:T(8,128)}), f32[512,512]{1,0:T(8,128)}) %all-gather.6.cloned.1.call-update) | async-done | bytes 1048592 | tf_op jit(solution)/shard_map/all_gather | solution.py:184
  569.3 271.1 %reduce-scatter.8.cloned.1.call-done = f32[128,8192]{0,1:T(8,128)} async-done(((f32[512,8192]{0,1:T(8,128)}), f32[128,8192]{0,1:T(8,128)}) %reduce-scatter.8.cloned.1.call-update) | async-done | bytes 4194320 | tf_op jit(solution)/shard_map/reduce_scatter | solution.py:168
  840.5 283.5 %reduce-scatter.6.cloned.1.call-done = f32[128,8192]{0,1:T(8,128)} async-done(((f32[512,8192]{0,1:T(8,128)}), f32[128,8192]{0,1:T(8,128)}) %reduce-scatter.6.cloned.1.call-update) | async-done | bytes 4194320 | tf_op jit(solution)/shard_map/reduce_scatter | solution.py:131
  1124.0 10.4 convert_multiply_fusion
  1139.3 2.6 reduce_sum.148
  1142.6 40.9 %all-reduce.1 = (f32[1]{0:T(128)}, f32[1]{0:T(128)}, f32[]{:T(128)}) all-reduce(f32[1]{0:T(128)} %bitcast.29, f32[1]{0:T(128)} %bitcast.28, f32[]{:T(128)S(6)} %mul.265), channel_id=1, replica_groups=mesh['dp'=8,'mp'=4] {'dp','mp'}, use_global_device_ids=true, to_apply=%region_5.0 | all-reduce | flops 3 | bytes 24 | tf_op jit(solution)/shard_map/psum | solution.py:135
  1186.0 4.1 copy.44
  1190.1 2.9 copy.43
  1193.0 2.8 all-reduce.4.cloned.1.call-done
  (117 shorter events, 46.7 us)
Async XLA Ops:
  7.2 555.7 %copy-start = (f32[128,512]{1,0:T(8,128)S(1)}, f32[128,512]{1,0:T(8,128)}, u32[]{:S(2)}) copy-start(f32[128,512]{1,0:T(8,128)} %param.30) | copy-start | bytes 786436
  7.2 402.0 %all-gather.4.cloned.1.call-start = ((), (), s32[]{:S(2)}) async-start(), calls=%async_computation.4 | async-start | bytes 10485760 | tf_op jit(solution)/shard_map/all_gather | solution.py:127
  21.8 2.2 copy-start.4
  23.9 436.3 %reduce-scatter.12.cloned.1.call-start = ((), (), s32[]{:S(2)}) async-start(), calls=%async_computation.9 | async-start | bytes 294912 | tf_op jit(solution)/shard_map/reduce_scatter | solution.py:176
  27.4 118.0 %copy-start.2 = (bf16[128,8192]{0,1:T(8,128)(2,1)}, bf16[128,8192]{0,1:T(8,128)(2,1)S(1)}, u32[]{:S(2)}) copy-start(bf16[128,8192]{0,1:T(8,128)(2,1)S(1)} %copy.41) | copy-start | bytes 6291460
  29.8 115.6 %copy-start.5 = (bf16[128,8192]{0,1:T(8,128)(2,1)}, bf16[128,8192]{0,1:T(8,128)(2,1)S(1)}, u32[]{:S(2)}) copy-start(bf16[128,8192]{0,1:T(8,128)(2,1)S(1)} %get-tuple-element.84) | copy-start | bytes 6291460
  29.8 115.7 %copy-start.14 = (f32[64,128]{1,0:T(8,128)S(1)}, f32[64,128]{1,0:T(8,128)}, u32[]{:S(2)}) copy-start(f32[64,128]{1,0:T(8,128)} %param.22) | copy-start | bytes 98308
  29.8 115.7 %copy-start.13 = (f32[128,64]{0,1:T(8,128)S(1)}, f32[128,64]{0,1:T(8,128)}, u32[]{:S(2)}) copy-start(f32[128,64]{0,1:T(8,128)} %param.23) | copy-start | bytes 98308
  29.8 113.0 %collective-permute-start = (bf16[128,8192]{0,1:T(8,128)(2,1)S(1)}, bf16[128,8192]{0,1:T(8,128)(2,1)S(1)}, u32[]{:S(2)}, u32[]{:S(2)}) collective-permute-start(bf16[128,8192]{0,1:T(8,128)(2,1)S(1)} %get-tuple-element.84), channel_id=1, source_target_pairs={{0,3},{1,0},{2,1},{3,2},{4,7},{5,4},{6,5},{7,6},{8,11},{9,8},{10,9... | collective-permute-start | bytes 6291464 | tf_op jit(solution)/shard_map/ppermute | solution.py:152
  142.8 2.6 copy-start.7
  145.4 250.7 %collective-permute-start.1 = (bf16[256,8192]{0,1:T(8,128)(2,1)}, bf16[256,8192]{0,1:T(8,128)(2,1)}, u32[]{:S(2)}, u32[]{:S(2)}) collective-permute-start(bf16[256,8192]{0,1:T(8,128)(2,1)} %pad_maximum_fusion), channel_id=1, source_target_pairs={{0,2},{1,3},{2,0},{3,1},{4,6},{5,7},{6,4},{7,5},{8,10},{9,11},{10,... | collective-permute-start | bytes 12582920 | tf_op jit(solution)/shard_map/ppermute | solution.py:152
  168.2 232.4 %copy-start.6 = (bf16[128,8192]{0,1:T(8,128)(2,1)S(1)}, bf16[128,8192]{0,1:T(8,128)(2,1)}, u32[]{:S(2)}) copy-start(bf16[128,8192]{0,1:T(8,128)(2,1)} %copy-done.5) | copy-start | bytes 6291460
  400.7 2.3 copy-start.8
  409.1 8.2 copy-start.1
  429.2 68.5 %reduce-scatter.10.cloned.1.call-start = ((), (), s32[]{:S(2)}) async-start(), calls=%async_computation.7 | async-start | bytes 294912 | tf_op jit(solution)/shard_map/reduce_scatter | solution.py:175
  439.8 97.8 %all-gather.8.cloned.1.call-start = ((), (), s32[]{:S(2)}) async-start(), calls=%async_computation.10 | async-start | bytes 1310720 | tf_op jit(solution)/shard_map/all_gather | solution.py:185
  471.4 87.0 %all-gather.6.cloned.1.call-start = ((), (), s32[]{:S(2)}) async-start(), calls=%async_computation.8 | async-start | bytes 1310720 | tf_op jit(solution)/shard_map/all_gather | solution.py:184
  508.9 331.5 %reduce-scatter.8.cloned.1.call-start = ((), (), s32[]{:S(2)}) async-start(), calls=%async_computation.6 | async-start | bytes 20971520 | tf_op jit(solution)/shard_map/reduce_scatter | solution.py:168
  518.6 605.3 %reduce-scatter.6.cloned.1.call-start = ((), (), s32[]{:S(2)}) async-start(), calls=%async_computation.5 | async-start | bytes 20971520 | tf_op jit(solution)/shard_map/reduce_scatter | solution.py:131
  526.8 669.0 %all-reduce.4.cloned.1.call-start = ((), (), s32[]{:S(2)}) async-start(), calls=%async_computation.11 | async-start | bytes 196608
  532.3 5.2 copy-start.21
  532.3 7.6 copy-start.19
  532.3 26.1 %copy-start.20 = (f32[64,128]{1,0:T(8,128)S(1)}, f32[64,128]{1,0:T(8,128)}, u32[]{:S(2)}) copy-start(f32[64,128]{1,0:T(8,128)} %param.24) | copy-start | bytes 98308
  532.4 28.1 %copy-start.22 = (f32[64,128]{1,0:T(8,128)S(1)}, f32[64,128]{1,0:T(8,128)}, u32[]{:S(2)}) copy-start(f32[64,128]{1,0:T(8,128)} %param.25) | copy-start | bytes 98308
  534.8 30.3 %copy-start.15 = (f32[64,512]{1,0:T(8,128)S(1)}, f32[64,512]{1,0:T(8,128)}, u32[]{:S(2)}) copy-start(f32[64,512]{1,0:T(8,128)} %param.31) | copy-start | bytes 393220
  534.8 31.1 %copy-start.16 = (f32[64,512]{1,0:T(8,128)S(1)}, f32[64,512]{1,0:T(8,128)}, u32[]{:S(2)}) copy-start(f32[64,512]{1,0:T(8,128)} %param.28) | copy-start | bytes 393220
  534.8 33.5 %copy-start.11 = (f32[128,512]{1,0:T(8,128)S(1)}, f32[128,512]{1,0:T(8,128)}, u32[]{:S(2)}) copy-start(f32[128,512]{1,0:T(8,128)} %param.29) | copy-start | bytes 786436
  534.8 589.2 %copy-start.3 = (bf16[128,8192]{0,1:T(8,128)(2,1)S(1)}, bf16[128,8192]{0,1:T(8,128)(2,1)}, u32[]{:S(2)}) copy-start(bf16[128,8192]{0,1:T(8,128)(2,1)} %copy-done.2) | copy-start | bytes 6291460
  1139.3 50.9 %copy-start.10 = (bf16[128,8192]{0,1:T(8,128)(2,1)S(1)}, bf16[128,8192]{0,1:T(8,128)(2,1)}, u32[]{:S(2)}) copy-start(bf16[128,8192]{0,1:T(8,128)(2,1)} %get-tuple-element.73) | copy-start | bytes 6291460
  1186.0 9.7 copy-start.18
  1186.0 9.7 copy-start.23
  1186.0 9.8 copy-start.24
  (4 other events, 4.7 us)
Sparse Core Ops, SparseCore 0:
  24.0 323.5 all-gather.3
  429.3 30.8 reduce-scatter.11
  464.1 33.5 reduce-scatter.9
  499.1 29.3 all-gather.7
  529.9 28.4 all-gather.5
  560.6 279.7 reduce-scatter.7
  842.9 281.0 reduce-scatter.5
  1142.7 53.0 all-reduce.3
